TPU v7x, 512 devices: a whole 4x8x8 slice. The times are simulated.
512 devices in a mesh: sec: 8 (over y), rad: 16 (over z, x_hi), ax: 4 (over x_lo, core).
Axes of the slice: x: 4 (x_hi: 2, x_lo: 2; x = x_hi * 2 + x_lo), y: 8, z: 8, core: 2. Of those that a mesh axis runs over, the one named last changes fastest.
Arguments:
- state: float32 [5, 8, 1024, 2048], P(None, 'ax', 'rad', 'sec'), may hold values from -1.6 to 4, as said below
- coarsen: int32 [16], replicated, may hold values from 1 to 16, as said below
Outputs:
- tendency: float32 [5, 8, 1024, 2048], P(None, 'ax', 'rad', 'sec')
Inputs may be any that keep to these rules, and one draw needn't show every extreme that they name: `coarsen`: each entry is a power of two; cycle 0 takes 16 and cycle 16 - 1 takes 1. state[0] (density) lies in 0.6 to 1.4, the momenta in -1.6 to 1.6, state[4] (energy) in 2.5 to 4.0.
All inputs are finite; a program needn't handle non-finite values.
Results may differ from a plain program's by a relative error of at most 0.0003.
Values sent between devices are 32-bit elements; how exact they have to be, the bound alone decides.
A program may use at most 64 MiB of HBM per device.

v0:
```python
import math
import jax
import jax.numpy as jnp
from jax import lax
from jax.sharding import PartitionSpec as P

R_NEAR = 16
GAMMA = 1.4
KAPPA = 1.44


def padded_2(value, sides, width):
    for axis, dim in sides:
        size, length = (lax.axis_size(axis), value.shape[dim])
        up = [(i, (i + 1) % size) for i in range(size)]
        down = [(j, i) for i, j in up]
        last = lax.slice_in_dim(value, length - width, length, axis=dim)
        first = lax.slice_in_dim(value, 0, width, axis=dim)
        before = lax.ppermute(last, axis, up)
        after = lax.ppermute(first, axis, down)
        value = jnp.concatenate([before, value, after], axis=dim)
    return value


def spread(value, axis, root):
    mine = lax.axis_index(axis) == root
    return lax.psum(jnp.where(mine, value, jnp.zeros_like(value)), axis)


def body(state, coarsen):
    fields, planes, cycles_dev, cells_dev = state.shape
    sec_count = lax.axis_size("sec")
    rad_count = lax.axis_size("rad")
    ax_count = lax.axis_size("ax")
    sec_index = lax.axis_index("sec")
    rad_index = lax.axis_index("rad")
    ax_index = lax.axis_index("ax")
    total_cells = cells_dev * sec_count
    dtheta = 2.0 * math.pi / total_cells
    padded = padded_2(state, (("sec", 3), ("rad", 2), ("ax", 1)), 1)
    plane_pos = ax_index * planes + jnp.arange(-1, planes + 1, dtype=jnp.int32)
    cycle_pos = rad_index * cycles_dev + jnp.arange(-1, cycles_dev + 1, dtype=jnp.int32)
    inside_ax = ((plane_pos >= 0) & (plane_pos < planes * ax_count)).astype(jnp.float32)
    inside_rad = ((cycle_pos >= 0) & (cycle_pos < cycles_dev * rad_count)).astype(jnp.float32)
    ghost_plane = jnp.arange(planes + 2) % (planes + 1) == 0
    ghost_cycle = jnp.arange(cycles_dev + 2) % (cycles_dev + 1) == 0
    ghost_cell = jnp.arange(cells_dev + 2) % (cells_dev + 1) == 0
    ghosts = (
        ghost_plane.astype(jnp.int32)[:, None, None]
        + ghost_cycle.astype(jnp.int32)[None, :, None]
        + ghost_cell.astype(jnp.int32)[None, None, :]
    )
    corner = ghosts >= 2
    density = jnp.where(corner, 1.0, padded[0])
    mom_ax = padded[1]
    mom_rad = padded[2]
    mom_az = padded[3]
    energy = padded[4]
    vel_ax = mom_ax / density
    vel_rad = mom_rad / density
    vel_az = mom_az / density
    pressure = (GAMMA - 1.0) * (
        energy - 0.5 * (mom_ax * vel_ax + mom_rad * vel_rad + mom_az * vel_az)
    )
    radius_pad = cycle_pos.astype(jnp.float32) + 0.5
    flux_ax = jnp.stack(
        [
            mom_ax,
            mom_ax * vel_ax + pressure,
            mom_rad * vel_ax,
            mom_az * vel_ax,
            (energy + pressure) * vel_ax,
        ]
    )
    flux_ax = flux_ax * inside_ax[None, :, None, None]
    flux_rad = jnp.stack(
        [
            mom_rad,
            mom_ax * vel_rad,
            mom_rad * vel_rad + pressure,
            mom_az * vel_rad,
            (energy + pressure) * vel_rad,
        ]
    )
    flux_rad = flux_rad * (radius_pad * inside_rad)[None, None, :, None]
    flux_az = jnp.stack(
        [
            mom_az,
            mom_ax * vel_az,
            mom_rad * vel_az,
            mom_az * vel_az + pressure,
            (energy + pressure) * vel_az,
        ]
    )
    radius = radius_pad[1:-1][:, None]
    tendency = -(flux_ax[:, 2:, 1:-1, 1:-1] - flux_ax[:, :-2, 1:-1, 1:-1]) * 0.5
    tendency = (
        tendency - (flux_rad[:, 1:-1, 2:, 1:-1] - flux_rad[:, 1:-1, :-2, 1:-1]) * 0.5 / radius
    )
    tendency = tendency - (flux_az[:, 1:-1, 1:-1, 2:] - flux_az[:, 1:-1, 1:-1, :-2]) * 0.5 / (
        radius * dtheta
    )
    inner_press = pressure[1:-1, 1:-1, 1:-1]
    inner_mom_az = mom_az[1:-1, 1:-1, 1:-1]
    inner_mom_rad = mom_rad[1:-1, 1:-1, 1:-1]
    inner_vel_az = vel_az[1:-1, 1:-1, 1:-1]
    zero_part = jnp.zeros_like(inner_press)
    source = jnp.stack(
        [
            zero_part,
            zero_part,
            (inner_press + inner_mom_az * inner_vel_az) / radius,
            -(inner_mom_rad * inner_vel_az) / radius,
            zero_part,
        ]
    )
    tendency = tendency + source
    own_pos = sec_index * cells_dev + jnp.arange(cells_dev, dtype=jnp.int32)

    def kernel(cycle_factor, cycle_blocks, log_ratio, scale_const, columns):
        rows_coarse = own_pos // cycle_factor
        columns_coarse = columns // cycle_factor
        distance = ((rows_coarse[:, None] - columns_coarse[None, :]) % cycle_blocks).astype(
            jnp.float32
        )
        blocks_f = cycle_blocks.astype(jnp.float32)
        return (jnp.exp(distance * log_ratio) + jnp.exp((blocks_f - distance) * log_ratio)) / (
            scale_const * cycle_factor.astype(jnp.float32)
        )

    near_axis = tendency[:, :, :R_NEAR, :]
    cycle_lines = jnp.transpose(near_axis, (2, 0, 1, 3)).reshape(R_NEAR, fields * planes, cells_dev)
    shared = spread(cycle_lines, "rad", 0)
    per_device = R_NEAR // rad_count
    my_cycles = lax.dynamic_slice_in_dim(shared, rad_index * per_device, per_device, 0)
    selector = (rad_index * per_device + jnp.arange(per_device, dtype=jnp.int32))[
        :, None
    ] == jnp.arange(coarsen.shape[0], dtype=jnp.int32)[None, :]
    factor = jnp.sum(jnp.where(selector, coarsen[None, :], 0), axis=1)
    blocks = total_cells // factor
    factor_f = factor.astype(jnp.float32)
    stiffness = KAPPA / (factor_f * dtheta) ** 2
    inverse_half = 0.5 / stiffness
    one_minus = jnp.sqrt(inverse_half * (2.0 + inverse_half)) - inverse_half
    log_ratio = jnp.log1p(-one_minus)
    scale_const = (
        stiffness
        * one_minus
        * (2.0 - one_minus)
        / (1.0 - one_minus)
        * -jnp.expm1(blocks.astype(jnp.float32) * log_ratio)
    )
    portion = lax.all_gather(my_cycles, "sec", axis=2, tiled=True)
    columns = jnp.arange(portion.shape[2], dtype=jnp.int32)

    def per_cycle(cycle_item):
        lines_one, cycle_factor, cycle_blocks, cycle_log, cycle_scale = cycle_item
        table = kernel(cycle_factor, cycle_blocks, cycle_log, cycle_scale, columns)
        return jnp.einsum("lq,pq->lp", lines_one, table, precision=lax.Precision.HIGHEST)

    smoothed = lax.map(per_cycle, (portion, factor, blocks, log_ratio, scale_const))
    result = lax.all_gather(smoothed, "rad", axis=0, tiled=True)
    restored = jnp.transpose(result.reshape(R_NEAR, fields, planes, cells_dev), (1, 2, 0, 3))
    near_new = jnp.where(rad_index == 0, restored, near_axis)
    return jnp.concatenate([near_new, tendency[:, :, R_NEAR:, :]], axis=2)


def solution(mesh):
    return jax.shard_map(
        body,
        mesh=mesh,
        in_specs=(P(None, "ax", "rad", "sec"), P()),
        out_specs=P(None, "ax", "rad", "sec"),
        check_vma=False,
    )
```

profile of v0, /device:TPU:6, one launch (start us, length us, event | category | flops | bytes accessed | tf_op | source)
XLA Modules:
  0.0 309.1 jit_solution(6789559779002969412)
XLA Ops:
  6.5 1.3 fusion.47
  7.8 3.5 %collective-permute-start = (f32[5,2,64,1]{3,2,1,0:T(8,128)S(1)}, f32[5,2,64,1]{3,2,1,0:T(8,128)S(1)}, u32[]{:S(2)}, u32[]{:S(2)}) collective-permute-start(f32[5,2,64,1]{3,2,1,0:T(8,128)S(1)} %get-tuple-element.59), channel_id=1, source_target_pairs={{0,64},{64,128},{128,192},{192,256},{256,320},{320,384},{384,448},... | collective-permute-start | bytes 7688 | tf_op jit(solution)/shard_map/ppermute | solution.py:19
  11.3 3.8 %collective-permute-start.1 = (f32[5,2,64,1]{3,2,1,0:T(8,128)S(1)}, f32[5,2,64,1]{3,2,1,0:T(8,128)S(1)}, u32[]{:S(2)}, u32[]{:S(2)}) collective-permute-start(f32[5,2,64,1]{3,2,1,0:T(8,128)S(1)} %get-tuple-element.60), channel_id=1, source_target_pairs={{64,0},{128,64},{192,128},{256,192},{320,256},{384,320},{448,384},... | collective-permute-start | bytes 7688 | tf_op jit(solution)/shard_map/ppermute | solution.py:20
  15.2 1.4 fusion.44
  16.6 4.3 %collective-permute-done = f32[5,2,64,1]{3,2,1,0:T(8,128)S(1)} collective-permute-done((f32[5,2,64,1]{3,2,1,0:T(8,128)S(1)}, f32[5,2,64,1]{3,2,1,0:T(8,128)S(1)}, u32[]{:S(2)}, u32[]{:S(2)}) %collective-permute-start) | collective-permute-done | bytes 2592 | tf_op jit(solution)/shard_map/ppermute | solution.py:19
  20.9 1.5 collective-permute-done.1
  22.4 1.1 pad_maximum_fusion.5
  23.5 5.1 %collective-permute-start.2 = (f32[5,2,1,258]{3,2,1,0:T(1,128)S(1)}, f32[5,2,1,258]{3,2,1,0:T(1,128)S(1)}, u32[]{:S(2)}, u32[]{:S(2)}) collective-permute-start(f32[5,2,1,258]{3,2,1,0:T(1,128)S(1)} %get-tuple-element.53), channel_id=1, source_target_pairs={{0,4},{4,8},{8,12},{12,16},{16,20},{20,24},{24,28},{28,32},{32,36}... | collective-permute-start | bytes 30968 | tf_op jit(solution)/shard_map/ppermute | solution.py:19
  28.6 2.2 collective-permute-start.3
  30.9 5.8 %collective-permute-done.3 = f32[5,2,1,258]{3,2,1,0:T(1,128)S(1)} collective-permute-done((f32[5,2,1,258]{3,2,1,0:T(1,128)S(1)}, f32[5,2,1,258]{3,2,1,0:T(1,128)S(1)}, u32[]{:S(2)}, u32[]{:S(2)}) %collective-permute-start.3) | collective-permute-done | bytes 10352 | tf_op jit(solution)/shard_map/ppermute | solution.py:20
  36.6 0.5 pad_maximum_fusion.1
  37.2 0.5 copy.5
  37.7 1.9 collective-permute-start.4
  39.6 0.5 copy.6
  40.2 3.6 %collective-permute-start.5 = (f32[5,1,66,258]{3,1,2,0:T(1,128)S(1)}, f32[5,1,66,258]{3,1,2,0:T(1,128)S(1)}, u32[]{:S(2)}, u32[]{:S(2)}) collective-permute-start(f32[5,1,66,258]{3,1,2,0:T(1,128)S(1)} %copy.6), channel_id=1, source_target_pairs={{1,0},{2,1},{3,2},{0,3},{5,4},{6,5},{7,6},{4,7},{9,8},{10,9},{11,1... | collective-permute-start | bytes 1021688 | tf_op jit(solution)/shard_map/ppermute | solution.py:20
  44.7 6.0 %collective-permute-done.4 = f32[5,1,66,258]{3,1,2,0:T(1,128)S(1)} collective-permute-done((f32[5,1,66,258]{3,1,2,0:T(1,128)S(1)}, f32[5,1,66,258]{3,1,2,0:T(1,128)S(1)}, u32[]{:S(2)}, u32[]{:S(2)}) %collective-permute-start.4) | collective-permute-done | bytes 340592 | tf_op jit(solution)/shard_map/ppermute | solution.py:19
  51.0 0.5 pad_maximum_fusion
  51.5 0.2 slice_bitcast_fusion.3
  51.9 0.3 add_dynamic-update-slice_fusion.2
  52.5 0.2 multiply_dynamic-update-slice_fusion.6
  52.9 0.4 broadcast_multiply_fusion
  53.3 0.3 fusion.32
  53.6 1.1 fusion.19
  54.7 0.7 slice_select_fusion.1
  55.4 0.8 and_select_fusion
  58.5 0.8 add_select_fusion.1
  59.4 161.4 %all-reduce.2.cloned.1.call-done = f32[16,10,256]{2,0,1:T(8,128)} async-done(((f32[16,10,256]{2,0,1:T(8,128)}), f32[16,10,256]{2,0,1:T(8,128)}) %all-reduce.2.cloned.1.call-update) | async-done | bytes 163856 | tf_op jit(solution)/shard_map/psum | solution.py:27
  220.8 0.9 constant_dynamic-slice_fusion
  221.7 16.7 %all_gather.6 = f32[1,10,2048]{2,0,1:T(1,128)S(1)} all-gather(f32[1,10,256]{2,0,1:T(1,128)S(1)} %constant_dynamic-slice_fusion), channel_id=1, replica_groups=mesh['sec'=8,'rad'=16,'ax'=4] {'sec'}, dimensions={2}, use_global_device_ids=true | all-gather | bytes 92160 | tf_op jit(solution)/shard_map/all_gather | solution.py:153
  238.4 22.6 %fusion.7 = f32[1,10,256]{2,1,0:T(8,128)S(1)} fusion(f32[]{:T(128)S(6)} %mul.233, f32[]{:T(128)S(6)} %convert_element_type.66, f32[]{:T(128)} %bitcast.13, s32[]{:T(128)S(6)} %select_n.132, s32[2048]{0:T(1024)S(1)} %add_select_fusion.1, s32[256]{0:T(256)S(1)} %and_select_fusion, pred[]{:T(512)S(6)} %lt.63, f32[1,10,2048]{2,0,1:T(1,128)S(1)} %all_gather.6), kind=kOutput, calls=%fused_computation.10 | convolution fusion | flops 70254592 | bytes 101393 | tf_op jit(solution)/shard_map/while/body/eval_jaxpr/lq,pq->lp/dot_general | solution.py:159
  261.0 40.3 %all-gather.1 = f32[16,10,256]{2,1,0:T(8,128)S(1)} all-gather(f32[1,10,256]{2,1,0:T(8,128)S(1)} %fusion.7), channel_id=2, replica_groups=mesh['sec'=8,'rad'=16,'ax'=4] {'rad'}, dimensions={0}, use_global_device_ids=true | all-gather | bytes 174080 | tf_op jit(solution)/shard_map/all_gather | solution.py:162
  301.4 0.9 pad_maximum_fusion.2
  (30 shorter events, 1.4 us)
Async XLA Ops:
  6.5 30.1 %copy-start = (f32[5,2,64,256]{3,2,1,0:T(8,128)S(1)}, f32[5,2,64,256]{3,2,1,0:T(8,128)}, u32[]{:S(2)}) copy-start(f32[5,2,64,256]{3,2,1,0:T(8,128)} %param.2) | copy-start | bytes 1966084
  6.5 214.2 %all-reduce.2.cloned.1.call-start = ((), (), s32[]{:S(2)}) async-start(), calls=%async_computation | async-start | bytes 327680 | tf_op jit(solution)/shard_map/psum | solution.py:27
  7.8 13.1 %collective-permute-start = (f32[5,2,64,1]{3,2,1,0:T(8,128)S(1)}, f32[5,2,64,1]{3,2,1,0:T(8,128)S(1)}, u32[]{:S(2)}, u32[]{:S(2)}) collective-permute-start(f32[5,2,64,1]{3,2,1,0:T(8,128)S(1)} %get-tuple-element.59), channel_id=1, source_target_pairs={{0,64},{64,128},{128,192},{192,256},{256,320},{320,384},{384,448},... | collective-permute-start | bytes 7688 | tf_op jit(solution)/shard_map/ppermute | solution.py:19
  11.3 11.1 %collective-permute-start.1 = (f32[5,2,64,1]{3,2,1,0:T(8,128)S(1)}, f32[5,2,64,1]{3,2,1,0:T(8,128)S(1)}, u32[]{:S(2)}, u32[]{:S(2)}) collective-permute-start(f32[5,2,64,1]{3,2,1,0:T(8,128)S(1)} %get-tuple-element.60), channel_id=1, source_target_pairs={{64,0},{128,64},{192,128},{256,192},{320,256},{384,320},{448,384},... | collective-permute-start | bytes 7688 | tf_op jit(solution)/shard_map/ppermute | solution.py:20
  23.5 7.4 %collective-permute-start.2 = (f32[5,2,1,258]{3,2,1,0:T(1,128)S(1)}, f32[5,2,1,258]{3,2,1,0:T(1,128)S(1)}, u32[]{:S(2)}, u32[]{:S(2)}) collective-permute-start(f32[5,2,1,258]{3,2,1,0:T(1,128)S(1)} %get-tuple-element.53), channel_id=1, source_target_pairs={{0,4},{4,8},{8,12},{12,16},{16,20},{20,24},{24,28},{28,32},{32,36}... | collective-permute-start | bytes 30968 | tf_op jit(solution)/shard_map/ppermute | solution.py:19
  28.6 8.0 %collective-permute-start.3 = (f32[5,2,1,258]{3,2,1,0:T(1,128)S(1)}, f32[5,2,1,258]{3,2,1,0:T(1,128)S(1)}, u32[]{:S(2)}, u32[]{:S(2)}) collective-permute-start(f32[5,2,1,258]{3,2,1,0:T(1,128)S(1)} %get-tuple-element.54), channel_id=1, source_target_pairs={{4,0},{8,4},{12,8},{16,12},{20,16},{24,20},{28,24},{32,28},{36,32}... | collective-permute-start | bytes 30968 | tf_op jit(solution)/shard_map/ppermute | solution.py:20
  37.7 13.0 %collective-permute-start.4 = (f32[5,1,66,258]{3,1,2,0:T(1,128)S(1)}, f32[5,1,66,258]{3,1,2,0:T(1,128)S(1)}, u32[]{:S(2)}, u32[]{:S(2)}) collective-permute-start(f32[5,1,66,258]{3,1,2,0:T(1,128)S(1)} %copy.5), channel_id=1, source_target_pairs={{0,1},{1,2},{2,3},{3,0},{4,5},{5,6},{6,7},{7,4},{8,9},{9,10},{10,1... | collective-permute-start | bytes 1021688 | tf_op jit(solution)/shard_map/ppermute | solution.py:19
  40.2 10.7 %collective-permute-start.5 = (f32[5,1,66,258]{3,1,2,0:T(1,128)S(1)}, f32[5,1,66,258]{3,1,2,0:T(1,128)S(1)}, u32[]{:S(2)}, u32[]{:S(2)}) collective-permute-start(f32[5,1,66,258]{3,1,2,0:T(1,128)S(1)} %copy.6), channel_id=1, source_target_pairs={{1,0},{2,1},{3,2},{0,3},{5,4},{6,5},{7,6},{4,7},{9,8},{10,9},{11,1... | collective-permute-start | bytes 1021688 | tf_op jit(solution)/shard_map/ppermute | solution.py:20
Sparse Core Ops, SparseCore 0:
  55.5 165.2 all-reduce.1
where the time goes:
time: 310 us; the launch traced here: 309 us
  waiting for transfers between devices  179 us (58%)
  blocking collectives  57 us (18%)
  matrix products  22.6 us (7%)
  starting transfers between devices  20.2 us (7%)
  between operations  16.7 us (5%)
  other arithmetic  9.79 us (3%)
  local copies, waits for them, and re-layouts  3.82 us (1%)
    psum x1, waiting for transfers between devices, spread(): return lax.psum(jnp.where(mine, value, jnp.zeros_like(value)), axis)  161 us
    all_gather x1, blocking collectives, body(): result = lax.all_gather(smoothed, 'rad', axis=0, tiled=True)  40.3 us
    dot_general x1, matrix products, per_cycle(): jnp.einsum('lq,pq->lp', lines_one, table, precision=lax.Precision.HIGHEST)  22.6 us
    all_gather x1, blocking collectives, body(): portion = lax.all_gather(my_cycles, 'sec', axis=2, tiled=True)  16.7 us
    ppermute x3, starting transfers between devices, padded_2(): before = lax.ppermute(last, axis, up)  10.5 us
    ppermute x3, waiting for transfers between devices, padded_2(): before = lax.ppermute(last, axis, up)  10.3 us
    ppermute x3, starting transfers between devices, padded_2(): after = lax.ppermute(first, axis, down)  9.68 us
    ppermute x3, waiting for transfers between devices, padded_2(): after = lax.ppermute(first, axis, down)  7.38 us
  transfers between devices with their start and end apart: 7, of which 6 were waited for; matrix products, arithmetic and copies ran while one was open for 1% of the time, Pallas kernels for 0%

commit v1 on v0

--- a/solution.py
+++ b/solution.py
@@ -150,7 +150,12 @@
         / (1.0 - one_minus)
         * -jnp.expm1(blocks.astype(jnp.float32) * log_ratio)
     )
-    portion = lax.all_gather(my_cycles, "sec", axis=2, tiled=True)
+    ring = [my_cycles]
+    for hop in range(7):
+        ring.append(lax.ppermute(ring[-1], "sec", [(dev, (dev + 1) % 8) for dev in range(8)]))
+    portion = jnp.roll(
+        jnp.concatenate(ring[::-1], axis=2), (lax.axis_index("sec") + 1) * ring[0].shape[2], axis=2
+    )
     columns = jnp.arange(portion.shape[2], dtype=jnp.int32)
 
     def per_cycle(cycle_item):

time: 310 us -> 343 us (1.11)
  waiting for transfers between devices: 179 us -> 212 us
  blocking collectives: 57 us -> 40.3 us
  starting transfers between devices: 20.2 us -> 35.5 us
    ppermute x0 -> x7, waiting for transfers between devices: none -> 26.9 us  [body(): lax.ppermute(ring[-1], 'sec', [(dev, (dev + 1) % 8) for dev in range(8)])]
    all_gather x1 -> x0, blocking collectives: 16.7 us -> none  [body(): portion = lax.all_gather(my_cycles, 'sec', axis=2, tiled=True)]
    ppermute x0 -> x7, starting transfers between devices: none -> 15.3 us  [body(): lax.ppermute(ring[-1], 'sec', [(dev, (dev + 1) % 8) for dev in range(8)])]
    psum x1, waiting for transfers between devices: 161 us -> 165 us  [spread(): return lax.psum(jnp.where(mine, value, jnp.zeros_like(value)), axis)]
  transfers between devices with their start and end apart: 7 -> 14, of which waited for: 6 -> 13; matrix products, arithmetic and copies ran while one was open for 1% -> 1% of each run, Pallas kernels for 0% -> 0%
where the time goes in v1:
time: 343 us; the launch traced here: 342 us
  waiting for transfers between devices  212 us (62%)
  blocking collectives  40.3 us (12%)
  starting transfers between devices  35.5 us (10%)
  matrix products  22.6 us (7%)
  between operations  16.6 us (5%)
  other arithmetic  8.94 us (3%)
  local copies, waits for them, and re-layouts  5.82 us (2%)
    psum x1, waiting for transfers between devices, spread(): return lax.psum(jnp.where(mine, value, jnp.zeros_like(value)), axis)  165 us
    all_gather x1, blocking collectives, body(): result = lax.all_gather(smoothed, 'rad', axis=0, tiled=True)  40.3 us
    ppermute x7, waiting for transfers between devices, body(): lax.ppermute(ring[-1], 'sec', [(dev, (dev + 1) % 8) for dev in range(8)])  26.9 us
    dot_general x1, matrix products, per_cycle(): jnp.einsum('lq,pq->lp', lines_one, table, precision=lax.Precision.HIGHEST)  22.6 us
    ppermute x7, starting transfers between devices, body(): lax.ppermute(ring[-1], 'sec', [(dev, (dev + 1) % 8) for dev in range(8)])  15.3 us
    ppermute x3, waiting for transfers between devices, padded_2(): before = lax.ppermute(last, axis, up)  12.4 us
    ppermute x3, starting transfers between devices, padded_2(): before = lax.ppermute(last, axis, up)  10.5 us
    ppermute x3, starting transfers between devices, padded_2(): after = lax.ppermute(first, axis, down)  9.68 us
  transfers between devices with their start and end apart: 14, of which 13 were waited for; matrix products, arithmetic and copies ran while one was open for 1% of the time, Pallas kernels for 0%

profile of v1, /device:TPU:6, one launch (start us, length us, event | category | flops | bytes accessed | tf_op | source)
XLA Modules:
  0.0 341.8 jit_solution(14723761056038695276)
XLA Ops:
  6.5 1.3 fusion.47
  7.8 3.5 %collective-permute-start = (f32[5,2,64,1]{3,2,1,0:T(8,128)S(1)}, f32[5,2,64,1]{3,2,1,0:T(8,128)S(1)}, u32[]{:S(2)}, u32[]{:S(2)}) collective-permute-start(f32[5,2,64,1]{3,2,1,0:T(8,128)S(1)} %get-tuple-element.59), channel_id=1, source_target_pairs={{0,64},{64,128},{128,192},{192,256},{256,320},{320,384},{384,448},... | collective-permute-start | bytes 7688 | tf_op jit(solution)/shard_map/ppermute | solution.py:19
  11.3 3.8 %collective-permute-start.1 = (f32[5,2,64,1]{3,2,1,0:T(8,128)S(1)}, f32[5,2,64,1]{3,2,1,0:T(8,128)S(1)}, u32[]{:S(2)}, u32[]{:S(2)}) collective-permute-start(f32[5,2,64,1]{3,2,1,0:T(8,128)S(1)} %get-tuple-element.60), channel_id=1, source_target_pairs={{64,0},{128,64},{192,128},{256,192},{320,256},{384,320},{448,384},... | collective-permute-start | bytes 7688 | tf_op jit(solution)/shard_map/ppermute | solution.py:20
  15.3 5.6 %collective-permute-done = f32[5,2,64,1]{3,2,1,0:T(8,128)S(1)} collective-permute-done((f32[5,2,64,1]{3,2,1,0:T(8,128)S(1)}, f32[5,2,64,1]{3,2,1,0:T(8,128)S(1)}, u32[]{:S(2)}, u32[]{:S(2)}) %collective-permute-start) | collective-permute-done | bytes 2592 | tf_op jit(solution)/shard_map/ppermute | solution.py:19
  20.9 1.5 collective-permute-done.1
  22.4 1.1 pad_maximum_fusion.5
  23.5 5.1 %collective-permute-start.2 = (f32[5,2,1,258]{3,2,1,0:T(1,128)S(1)}, f32[5,2,1,258]{3,2,1,0:T(1,128)S(1)}, u32[]{:S(2)}, u32[]{:S(2)}) collective-permute-start(f32[5,2,1,258]{3,2,1,0:T(1,128)S(1)} %get-tuple-element.53), channel_id=1, source_target_pairs={{0,4},{4,8},{8,12},{12,16},{16,20},{20,24},{24,28},{28,32},{32,36}... | collective-permute-start | bytes 30968 | tf_op jit(solution)/shard_map/ppermute | solution.py:19
  28.6 2.2 collective-permute-start.3
  30.9 5.8 %collective-permute-done.3 = f32[5,2,1,258]{3,2,1,0:T(1,128)S(1)} collective-permute-done((f32[5,2,1,258]{3,2,1,0:T(1,128)S(1)}, f32[5,2,1,258]{3,2,1,0:T(1,128)S(1)}, u32[]{:S(2)}, u32[]{:S(2)}) %collective-permute-start.3) | collective-permute-done | bytes 10352 | tf_op jit(solution)/shard_map/ppermute | solution.py:20
  37.7 1.9 collective-permute-start.4
  40.2 3.6 %collective-permute-start.5 = (f32[5,1,66,258]{3,1,2,0:T(1,128)S(1)}, f32[5,1,66,258]{3,1,2,0:T(1,128)S(1)}, u32[]{:S(2)}, u32[]{:S(2)}) collective-permute-start(f32[5,1,66,258]{3,1,2,0:T(1,128)S(1)} %copy.6), channel_id=1, source_target_pairs={{1,0},{2,1},{3,2},{0,3},{5,4},{6,5},{7,6},{4,7},{9,8},{10,9},{11,1... | collective-permute-start | bytes 1021688 | tf_op jit(solution)/shard_map/ppermute | solution.py:20
  44.0 6.7 %collective-permute-done.4 = f32[5,1,66,258]{3,1,2,0:T(1,128)S(1)} collective-permute-done((f32[5,1,66,258]{3,1,2,0:T(1,128)S(1)}, f32[5,1,66,258]{3,1,2,0:T(1,128)S(1)}, u32[]{:S(2)}, u32[]{:S(2)}) %collective-permute-start.4) | collective-permute-done | bytes 340592 | tf_op jit(solution)/shard_map/ppermute | solution.py:19
  53.6 1.1 fusion.19
  55.4 165.4 %all-reduce.2.cloned.1.call-done = f32[16,10,256]{2,0,1:T(8,128)} async-done(((f32[16,10,256]{2,0,1:T(8,128)}), f32[16,10,256]{2,0,1:T(8,128)}) %all-reduce.2.cloned.1.call-update) | async-done | bytes 163856 | tf_op jit(solution)/shard_map/psum | solution.py:27
  221.7 3.4 collective-permute-start.6
  225.1 3.4 collective-permute-done.6
  228.5 2.2 collective-permute-start.7
  230.6 4.6 %collective-permute-done.7 = f32[1,10,256]{2,0,1:T(1,128)S(1)} collective-permute-done((f32[1,10,256]{2,0,1:T(1,128)S(1)}, f32[1,10,256]{2,0,1:T(1,128)S(1)}, u32[]{:S(2)}, u32[]{:S(2)}) %collective-permute-start.7) | collective-permute-done | bytes 10272 | tf_op jit(solution)/shard_map/ppermute | solution.py:155
  235.2 1.9 collective-permute-start.8
  237.1 4.8 %collective-permute-done.8 = f32[1,10,256]{2,0,1:T(1,128)S(1)} collective-permute-done((f32[1,10,256]{2,0,1:T(1,128)S(1)}, f32[1,10,256]{2,0,1:T(1,128)S(1)}, u32[]{:S(2)}, u32[]{:S(2)}) %collective-permute-start.8) | collective-permute-done | bytes 10272 | tf_op jit(solution)/shard_map/ppermute | solution.py:155
  242.0 1.9 collective-permute-start.9
  243.9 4.8 %collective-permute-done.9 = f32[1,10,256]{2,0,1:T(1,128)S(1)} collective-permute-done((f32[1,10,256]{2,0,1:T(1,128)S(1)}, f32[1,10,256]{2,0,1:T(1,128)S(1)}, u32[]{:S(2)}, u32[]{:S(2)}) %collective-permute-start.9) | collective-permute-done | bytes 10272 | tf_op jit(solution)/shard_map/ppermute | solution.py:155
  248.8 1.9 collective-permute-start.10
  252.0 3.6 %collective-permute-done.10 = f32[1,10,256]{2,0,1:T(1,128)S(1)} collective-permute-done((f32[1,10,256]{2,0,1:T(1,128)S(1)}, f32[1,10,256]{2,0,1:T(1,128)S(1)}, u32[]{:S(2)}, u32[]{:S(2)}) %collective-permute-start.10) | collective-permute-done | bytes 10272 | tf_op jit(solution)/shard_map/ppermute | solution.py:155
  255.5 1.9 collective-permute-start.11
  258.2 4.1 %collective-permute-done.11 = f32[1,10,256]{2,0,1:T(1,128)S(1)} collective-permute-done((f32[1,10,256]{2,0,1:T(1,128)S(1)}, f32[1,10,256]{2,0,1:T(1,128)S(1)}, u32[]{:S(2)}, u32[]{:S(2)}) %collective-permute-start.11) | collective-permute-done | bytes 10272 | tf_op jit(solution)/shard_map/ppermute | solution.py:155
  262.3 2.1 collective-permute-start.12
  267.4 1.6 collective-permute-done.12
  269.1 0.9 constant_dynamic-update-slice_fusion.8
  270.2 0.9 constant_dynamic-update-slice_fusion
  271.1 22.6 %fusion.7 = f32[1,10,256]{2,1,0:T(8,128)S(1)} fusion(f32[]{:T(128)S(6)} %mul.237, f32[]{:T(128)S(6)} %convert_element_type.66, f32[]{:T(128)} %bitcast.13, s32[]{:T(128)S(6)} %select_n.146, s32[2048]{0:T(1024)S(1)} %add_select_fusion.1, s32[256]{0:T(256)S(1)} %and_select_fusion, pred[]{:T(512)S(6)} %lt.77, f32[1,10,2048]{2,0,1:T(1,128)S(1)} %constant_dynamic-slice_fusion), kind=kOutput, calls=%fused_computation.10 | convolution fusion | flops 70254592 | bytes 101393 | tf_op jit(solution)/shard_map/while/body/eval_jaxpr/lq,pq->lp/dot_general | solution.py:164
  293.7 40.3 %all-gather.1 = f32[16,10,256]{2,1,0:T(8,128)S(1)} all-gather(f32[1,10,256]{2,1,0:T(8,128)S(1)} %fusion.7), channel_id=2, replica_groups=mesh['sec'=8,'rad'=16,'ax'=4] {'rad'}, dimensions={0}, use_global_device_ids=true | all-gather | bytes 174080 | tf_op jit(solution)/shard_map/all_gather | solution.py:167
  (62 shorter events, 9.7 us)
Async XLA Ops:
  6.5 30.1 %copy-start = (f32[5,2,64,256]{3,2,1,0:T(8,128)S(1)}, f32[5,2,64,256]{3,2,1,0:T(8,128)}, u32[]{:S(2)}) copy-start(f32[5,2,64,256]{3,2,1,0:T(8,128)} %param.2) | copy-start | bytes 1966084
  6.5 214.2 %all-reduce.2.cloned.1.call-start = ((), (), s32[]{:S(2)}) async-start(), calls=%async_computation | async-start | bytes 327680 | tf_op jit(solution)/shard_map/psum | solution.py:27
  7.8 13.1 %collective-permute-start = (f32[5,2,64,1]{3,2,1,0:T(8,128)S(1)}, f32[5,2,64,1]{3,2,1,0:T(8,128)S(1)}, u32[]{:S(2)}, u32[]{:S(2)}) collective-permute-start(f32[5,2,64,1]{3,2,1,0:T(8,128)S(1)} %get-tuple-element.59), channel_id=1, source_target_pairs={{0,64},{64,128},{128,192},{192,256},{256,320},{320,384},{384,448},... | collective-permute-start | bytes 7688 | tf_op jit(solution)/shard_map/ppermute | solution.py:19
  11.3 11.1 %collective-permute-start.1 = (f32[5,2,64,1]{3,2,1,0:T(8,128)S(1)}, f32[5,2,64,1]{3,2,1,0:T(8,128)S(1)}, u32[]{:S(2)}, u32[]{:S(2)}) collective-permute-start(f32[5,2,64,1]{3,2,1,0:T(8,128)S(1)} %get-tuple-element.60), channel_id=1, source_target_pairs={{64,0},{128,64},{192,128},{256,192},{320,256},{384,320},{448,384},... | collective-permute-start | bytes 7688 | tf_op jit(solution)/shard_map/ppermute | solution.py:20
  23.5 7.4 %collective-permute-start.2 = (f32[5,2,1,258]{3,2,1,0:T(1,128)S(1)}, f32[5,2,1,258]{3,2,1,0:T(1,128)S(1)}, u32[]{:S(2)}, u32[]{:S(2)}) collective-permute-start(f32[5,2,1,258]{3,2,1,0:T(1,128)S(1)} %get-tuple-element.53), channel_id=1, source_target_pairs={{0,4},{4,8},{8,12},{12,16},{16,20},{20,24},{24,28},{28,32},{32,36}... | collective-permute-start | bytes 30968 | tf_op jit(solution)/shard_map/ppermute | solution.py:19
  28.6 8.0 %collective-permute-start.3 = (f32[5,2,1,258]{3,2,1,0:T(1,128)S(1)}, f32[5,2,1,258]{3,2,1,0:T(1,128)S(1)}, u32[]{:S(2)}, u32[]{:S(2)}) collective-permute-start(f32[5,2,1,258]{3,2,1,0:T(1,128)S(1)} %get-tuple-element.54), channel_id=1, source_target_pairs={{4,0},{8,4},{12,8},{16,12},{20,16},{24,20},{28,24},{32,28},{36,32}... | collective-permute-start | bytes 30968 | tf_op jit(solution)/shard_map/ppermute | solution.py:20
  37.7 13.0 %collective-permute-start.4 = (f32[5,1,66,258]{3,1,2,0:T(1,128)S(1)}, f32[5,1,66,258]{3,1,2,0:T(1,128)S(1)}, u32[]{:S(2)}, u32[]{:S(2)}) collective-permute-start(f32[5,1,66,258]{3,1,2,0:T(1,128)S(1)} %copy.5), channel_id=1, source_target_pairs={{0,1},{1,2},{2,3},{3,0},{4,5},{5,6},{6,7},{7,4},{8,9},{9,10},{10,1... | collective-permute-start | bytes 1021688 | tf_op jit(solution)/shard_map/ppermute | solution.py:19
  40.2 10.7 %collective-permute-start.5 = (f32[5,1,66,258]{3,1,2,0:T(1,128)S(1)}, f32[5,1,66,258]{3,1,2,0:T(1,128)S(1)}, u32[]{:S(2)}, u32[]{:S(2)}) collective-permute-start(f32[5,1,66,258]{3,1,2,0:T(1,128)S(1)} %copy.6), channel_id=1, source_target_pairs={{1,0},{2,1},{3,2},{0,3},{5,4},{6,5},{7,6},{4,7},{9,8},{10,9},{11,1... | collective-permute-start | bytes 1021688 | tf_op jit(solution)/shard_map/ppermute | solution.py:20
  53.6 197.1 %copy-start.1 = (s32[16]{0:T(128)S(1)}, s32[16]{0:T(128)}, u32[]{:S(2)}) copy-start(s32[16]{0:T(128)} %param.3) | copy-start | bytes 196
  221.7 6.8 %collective-permute-start.6 = (f32[1,10,256]{2,0,1:T(1,128)S(1)}, f32[1,10,256]{2,0,1:T(1,128)S(1)}, u32[]{:S(2)}, u32[]{:S(2)}) collective-permute-start(f32[1,10,256]{2,0,1:T(1,128)S(1)} %constant_dynamic-slice_fusion.1), channel_id=1, source_target_pairs={{0,64},{64,128},{128,192},{192,256},{256,320},{320,384},{384,448},... | collective-permute-start | bytes 30728 | tf_op jit(solution)/shard_map/ppermute | solution.py:155
  228.5 6.8 %collective-permute-start.7 = (f32[1,10,256]{2,0,1:T(1,128)S(1)}, f32[1,10,256]{2,0,1:T(1,128)S(1)}, u32[]{:S(2)}, u32[]{:S(2)}) collective-permute-start(f32[1,10,256]{2,0,1:T(1,128)S(1)} %collective-permute-done.6), channel_id=1, source_target_pairs={{0,64},{64,128},{128,192},{192,256},{256,320},{320,384},{384,448},... | collective-permute-start | bytes 30728 | tf_op jit(solution)/shard_map/ppermute | solution.py:155
  235.2 6.8 %collective-permute-start.8 = (f32[1,10,256]{2,0,1:T(1,128)S(1)}, f32[1,10,256]{2,0,1:T(1,128)S(1)}, u32[]{:S(2)}, u32[]{:S(2)}) collective-permute-start(f32[1,10,256]{2,0,1:T(1,128)S(1)} %collective-permute-done.7), channel_id=1, source_target_pairs={{0,64},{64,128},{128,192},{192,256},{256,320},{320,384},{384,448},... | collective-permute-start | bytes 30728 | tf_op jit(solution)/shard_map/ppermute | solution.py:155
  242.0 6.8 %collective-permute-start.9 = (f32[1,10,256]{2,0,1:T(1,128)S(1)}, f32[1,10,256]{2,0,1:T(1,128)S(1)}, u32[]{:S(2)}, u32[]{:S(2)}) collective-permute-start(f32[1,10,256]{2,0,1:T(1,128)S(1)} %collective-permute-done.8), channel_id=1, source_target_pairs={{0,64},{64,128},{128,192},{192,256},{256,320},{320,384},{384,448},... | collective-permute-start | bytes 30728 | tf_op jit(solution)/shard_map/ppermute | solution.py:155
  248.8 6.8 %collective-permute-start.10 = (f32[1,10,256]{2,0,1:T(1,128)S(1)}, f32[1,10,256]{2,0,1:T(1,128)S(1)}, u32[]{:S(2)}, u32[]{:S(2)}) collective-permute-start(f32[1,10,256]{2,0,1:T(1,128)S(1)} %collective-permute-done.9), channel_id=1, source_target_pairs={{0,64},{64,128},{128,192},{192,256},{256,320},{320,384},{384,448},... | collective-permute-start | bytes 30728 | tf_op jit(solution)/shard_map/ppermute | solution.py:155
  255.5 6.8 %collective-permute-start.11 = (f32[1,10,256]{2,0,1:T(1,128)S(1)}, f32[1,10,256]{2,0,1:T(1,128)S(1)}, u32[]{:S(2)}, u32[]{:S(2)}) collective-permute-start(f32[1,10,256]{2,0,1:T(1,128)S(1)} %collective-permute-done.10), channel_id=1, source_target_pairs={{0,64},{64,128},{128,192},{192,256},{256,320},{320,384},{384,448},... | collective-permute-start | bytes 30728 | tf_op jit(solution)/shard_map/ppermute | solution.py:155
  262.3 6.8 %collective-permute-start.12 = (f32[1,10,256]{2,0,1:T(1,128)S(1)}, f32[1,10,256]{2,0,1:T(1,128)S(1)}, u32[]{:S(2)}, u32[]{:S(2)}) collective-permute-start(f32[1,10,256]{2,0,1:T(1,128)S(1)} %collective-permute-done.11), channel_id=1, source_target_pairs={{0,64},{64,128},{128,192},{192,256},{256,320},{320,384},{384,448},... | collective-permute-start | bytes 30728 | tf_op jit(solution)/shard_map/ppermute | solution.py:155
Sparse Core Ops, SparseCore 0:
  55.5 165.2 all-reduce.1
